TPU v7x, 32 devices: a whole 2x2x4 slice. The times are simulated.
32 devices in a mesh: pts: 8 (over z, y), freq: 4 (over x, core).
Axes of the slice: x: 2, y: 2, z: 4, core: 2. Of those that a mesh axis runs over, the one named last changes fastest.
Arguments:
- spectra: bfloat16 [64, 5, 2048, 128], P('freq', None, 'pts'), parts along dimension 0, may hold values from -200 to 200, as said below
- weights: float32 [2048], P('pts'), as said below
Outputs:
- mode_shapes: bfloat16 [64, 5, 2048, 128], P('freq', None, 'pts'), parts along dimension 0
There are 4 independent parts, one for each index of `freq`. A program takes and returns all parts, laid end to end along the dimension named above; an argument that names none is the same for every part. Nothing has to cross between parts.
Inputs may be any that keep to these rules, and one draw needn't show every extreme that they name: `spectra`: each row (frequency, variable, point) and each block's column pair has its own scale; the complex columns are independent. `weights`: Positive; their sum is of order one.
All inputs are finite; a program needn't handle non-finite values.
Results may differ from a plain program's by a relative error of at most 0.0054.
Values sent between devices are 32-bit elements; how exact they have to be, the bound alone decides.
A program may use at most 64 MiB of HBM per device.

v0:
```python
import jax
import jax.numpy as jnp
from jax import lax
from jax.sharding import PartitionSpec as P

NS_STEPS = 10


def split_parts(products):
    half_cols = products.shape[-1] // 2
    top_left = products[:, :half_cols, :half_cols]
    top_right = products[:, :half_cols, half_cols:]
    bottom_left = products[:, half_cols:, :half_cols]
    bottom_right = products[:, half_cols:, half_cols:]
    return (top_left + bottom_right, top_right - bottom_left)


def build_cross(real_part, imag_part):
    upper_row = jnp.concatenate([real_part, imag_part], 2)
    lower_row = jnp.concatenate([-imag_part, real_part], 2)
    return jnp.concatenate([upper_row, lower_row], 1)


def upper_of(cross_gram):
    order = cross_gram.shape[-1]
    places = jnp.arange(order)

    def eliminate(column, carry):
        working, factor = carry
        picker = (places == column).astype(jnp.float32)
        below = (places >= column).astype(jnp.float32)
        current = jnp.sum(working * picker[None, None, :], axis=2) * below[None, :]
        pivot = jnp.sqrt(jnp.sum(current * picker[None, :], axis=1))
        scaled = current / pivot[:, None]
        factor = factor + scaled[:, None, :] * picker[None, :, None]
        working = working - scaled[:, :, None] * scaled[:, None, :]
        return (working, factor)

    start = (cross_gram, jnp.zeros_like(cross_gram))
    working, factor = lax.fori_loop(0, order, eliminate, start)
    return factor


def solve_upper(upper_factor, right_side):
    order = upper_factor.shape[-1]
    places = jnp.arange(order)

    def back_step(count, solved):
        row = order - 1 - count
        picker = (places == row).astype(jnp.float32)
        factor_row = jnp.sum(upper_factor * picker[None, :, None], axis=1)
        side_row = jnp.sum(right_side * picker[None, :, None], axis=1)
        pivot = jnp.sum(factor_row * picker[None, :], axis=1)
        known = jnp.einsum("fj,fjk->fk", factor_row, solved, precision=lax.Precision.HIGHEST)
        value = (side_row - known) / pivot[:, None]
        return solved + picker[None, :, None] * value[:, None, :]

    return lax.fori_loop(0, order, back_step, jnp.zeros_like(right_side))


def gram_of(upper_factor):
    return jnp.einsum("fki,fkj->fij", upper_factor, upper_factor, precision=lax.Precision.HIGHEST)


def local(spectra, weights):
    freq_count, var_count, point_count, col_count = spectra.shape
    root_weights = jnp.sqrt(weights)
    weighted = (root_weights[None, None, :, None] * spectra.astype(jnp.float32)).astype(
        jnp.bfloat16
    )
    flat_rows = weighted.reshape(freq_count, var_count * point_count, col_count)
    products = jnp.einsum("frc,frd->fcd", flat_rows, flat_rows, preferred_element_type=jnp.float32)
    real_part, imag_part = split_parts(products)
    half_cols = col_count // 2
    row_place = jnp.arange(half_cols)[:, None]
    col_place = jnp.arange(half_cols)[None, :]
    upper_mask = (row_place <= col_place)[None]
    strict_upper = (row_place < col_place)[None]
    strict_lower = (row_place > col_place)[None]
    packed = jnp.where(upper_mask, real_part, imag_part)
    summed = lax.psum(packed, "pts")
    flipped = jnp.swapaxes(summed, 1, 2)
    real_full = jnp.where(upper_mask, summed, flipped)
    imag_full = jnp.where(strict_lower, summed, 0.0) - jnp.where(strict_upper, flipped, 0.0)
    upper_factor = upper_of(build_cross(real_full, imag_full))
    frob_norm = jnp.sqrt(jnp.sum(upper_factor * upper_factor, axis=(1, 2)))
    polar = upper_factor / frob_norm[:, None, None]
    for sweep in range(NS_STEPS):
        inner_gram = gram_of(polar)
        polar = 1.5 * polar - 0.5 * jnp.einsum(
            "fij,fjk->fik", polar, inner_gram, precision=lax.Precision.HIGHEST
        )
    mapping = solve_upper(upper_factor, polar).astype(jnp.bfloat16)
    shapes = jnp.einsum("fvpc,fcd->fvpd", spectra, mapping, preferred_element_type=jnp.float32)
    return shapes.astype(jnp.bfloat16)


def solution(mesh):
    in_specs = (P("freq", None, "pts", None), P("pts"))
    out_specs = P("freq", None, "pts", None)
    return jax.shard_map(local, mesh=mesh, in_specs=in_specs, out_specs=out_specs, check_vma=False)
```

profile of v0, /device:TPU:0, one launch (start us, length us, event | category | flops | bytes accessed | tf_op | source)
XLA Modules:
  0.0 513.6 jit_solution(6503362258523751041)
XLA Ops:
  7.2 4.0 multiply_convert_fusion
  11.3 1.6 fusion.26
  12.9 1.1 fusion.19
  14.1 75.1 %all-reduce.2.cloned.1.call-done = f32[16,64,64]{2,1,0:T(8,128)} async-done(((f32[16,64,64]{2,1,0:T(8,128)}), f32[16,64,64]{2,1,0:T(8,128)}) %all-reduce.2.cloned.1.call-update) | async-done | bytes 262160 | tf_op jit(solution)/shard_map/psum | solution.py:81
  89.3 1.2 copy.8
  90.5 1.2 fusion.24
  92.1 158.6 %while.32 = (s32[]{:T(128)}, f32[16,128,128]{2,1,0:T(8,128)S(1)}, f32[16,128,128]{2,1,0:T(8,128)S(1)}, s32[]{:T(128)}, s32[]{:T(128)}) while((s32[]{:T(128)}, f32[16,128,128]{2,1,0:T(8,128)S(1)}, f32[16,128,128]{2,1,0:T(8,128)S(1)}, s32[]{:T(128)}, s32[]{:T(128)}) %tuple.74), condition=%wide.region_4.5_spmd.clone.clone, body=%wide.region_1.4_spmd.clone.clone.sunk | while | flops 1843699 | bytes 5287763 | solution.py:40
  250.9 1.9 fusion.23
  252.9 1.4 fusion.18
  254.3 1.9 fusion.27
  256.2 1.3 fusion.17
  257.5 1.9 fusion.28
  259.4 1.3 fusion.16
  260.7 1.9 fusion.29
  262.6 1.5 fusion.15
  264.2 1.9 fusion.30
  266.1 1.3 fusion.14
  267.4 1.9 fusion.31
  269.3 1.3 fusion.13
  270.6 1.9 fusion.32
  272.6 1.3 fusion.12
  273.9 2.2 fusion.33
  276.1 1.3 fusion.11
  277.4 1.9 fusion.34
  279.3 1.3 fusion.10
  280.6 1.9 fusion.35
  282.5 1.3 fusion.9
  283.8 208.3 %while.31 = (s32[]{:T(128)}, f32[16,128,128]{2,1,0:T(8,128)S(1)}, f32[16,128,128]{2,1,0:T(8,128)S(1)}, f32[16,128,128]{2,1,0:T(8,128)S(1)}, s32[]{:T(128)}, /*index=5*/s32[]{:T(128)}, s32[]{:T(128)}) while((s32[]{:T(128)}, f32[16,128,128]{2,1,0:T(8,128)S(1)}, f32[16,128,128]{2,1,0:T(8,128)S(1)}, f32[16,128,128]{2,1,0:T(8,128)S(1)}, ...), condition=%wide.region_10.11_spmd.clone, body=%wide.region_6.10_spmd.clone.sunk | while | flops 5247220 | bytes 5318896 | solution.py:58
  284.2 0.9 fusion.82
  287.5 0.9 fusion.82
  289.1 0.9 fusion.82
  292.4 0.9 fusion.82
  295.6 0.9 fusion.82
  300.5 0.9 fusion.82
  303.8 0.9 fusion.82
  307.0 0.9 fusion.82
  308.6 0.9 fusion.82
  311.9 0.9 fusion.82
  315.1 0.9 fusion.82
  318.4 0.9 fusion.82
  320.0 0.9 fusion.82
  323.3 0.9 fusion.82
  326.5 0.9 fusion.82
  331.4 0.9 fusion.82
  334.7 0.9 fusion.82
  337.9 0.9 fusion.82
  492.1 6.4 %convert_bitcast_fusion = bf16[16,5,256,128]{2,3,1,0:T(8,128)(2,1)} fusion(bf16[16,5,256,128]{3,2,1,0:T(8,128)(2,1)} %param.6, f32[16,128,128]{2,1,0:T(8,128)S(1)} %get-tuple-element.182), kind=kOutput, calls=%fused_computation.21 | convolution fusion | flops 673972224 | bytes 11534336 | tf_op jit(solution)/shard_map/fvpc,fcd->fvpd/dot_general | solution.py:94
  498.5 7.8 %copy.10 = bf16[16,5,256,128]{3,2,1,0:T(8,128)(2,1)} copy(bf16[16,5,256,128]{2,3,1,0:T(8,128)(2,1)} %convert_bitcast_fusion) | data formatting | bytes 10485760 | tf_op jit(solution)/shard_map/convert_element_type | solution.py:95
  (1528 shorter events, 341.1 us)
Async XLA Ops:
  6.5 82.7 %all-reduce.2.cloned.1.call-start = ((), (), s32[]{:S(2)}) async-start(), calls=%async_computation | async-start | bytes 1048576 | tf_op jit(solution)/shard_map/psum | solution.py:81
Sparse Core Ops, SparseCore 0:
  14.2 75.0 all-reduce.1
where the time goes:
time: 518 us; the launch traced here: 514 us
  other arithmetic  243 us (47%)
  matrix products  160 us (31%)
  waiting for transfers between devices  75.2 us (15%)
  between operations  14 us (3%)
  local copies, waits for them, and re-layouts  10.8 us (2%)
  loops' own time  10.3 us (2%)
    dot_general x128, matrix products, back_step(): jnp.einsum('fj,fjk->fk', factor_row, solved, precision=lax.Precision.HIGH...  120 us
    add x128, other arithmetic, eliminate(): factor = factor + scaled[:, None, :] * picker[None, :, None]  82.9 us
    psum x1, waiting for transfers between devices, local(): summed = lax.psum(packed, 'pts')  75.1 us
    reduce_sum x128, other arithmetic, eliminate(): current = jnp.sum(working * picker[None, None, :], axis=2) * below[None, :]  44 us
    reduce_sum x128, other arithmetic, back_step(): factor_row = jnp.sum(upper_factor * picker[None, :, None], axis=1)  33.5 us
    add x128, other arithmetic, back_step(): return solved + picker[None, :, None] * value[:, None, :]  25.4 us
    dot_general x10, matrix products, gram_of(): jnp.einsum('fki,fkj->fij', upper_factor, upper_factor, precision=lax.Prec...  19.5 us
    reduce_sum x128, other arithmetic, eliminate(): pivot = jnp.sqrt(jnp.sum(current * picker[None, :], axis=1))  14.6 us
  transfers between devices with their start and end apart: 1, of which 1 were waited for; matrix products, arithmetic and copies ran while one was open for 0% of the time, Pallas kernels for 0%

commit v1 on v0

v1 whole, which is shorter than its diff:
```python
import functools

import jax
import jax.numpy as jnp
from jax import lax
from jax.experimental import pallas as pl
from jax.experimental.pallas import tpu as pltpu
from jax.sharding import PartitionSpec as P

NS_STEPS = 10
MESH = pl.DeviceIdType.MESH


def places(shape):
    return (
        lax.broadcasted_iota(jnp.int32, shape, 0),
        lax.broadcasted_iota(jnp.int32, shape, 1),
    )


def pack(top):
    half, cols = top.shape
    row, lane = places(top.shape)
    left = lane < half
    upper = jnp.where(left, lane, lane - half) >= row
    rolled = pltpu.roll(top, half, 1)
    both = jnp.where(jnp.logical_xor(left, upper), rolled, top)
    quarter = half // 2
    return jnp.where(left[:quarter], both[:quarter], both[quarter:])


def unpack(packed):
    quarter, cols = packed.shape
    half = 2 * quarter
    left = places(packed.shape)[1] < half
    rolled = pltpu.roll(packed, half, 1)
    top = jnp.where(left, packed, rolled)
    bottom = jnp.where(left, rolled, packed)
    full = jnp.concatenate([top, bottom, top, bottom], 0)
    flipped = full.T
    row, lane = places(full.shape)
    row_left, lane_left = row < half, lane < half
    i = jnp.where(row_left, row, row - half)
    j = jnp.where(lane_left, lane, lane - half)
    real = jnp.where(j >= i, full, flipped)
    imag = jnp.where(j < i, full, jnp.where(j > i, -flipped, 0.0))
    imag = jnp.where(row_left, imag, -imag)
    return jnp.where(jnp.logical_xor(row_left, lane_left), imag, real)


def split(a):
    high = a.astype(jnp.bfloat16)
    low = (a - high.astype(jnp.float32)).astype(jnp.bfloat16)
    return high, low


def left_form(a):
    high, low = split(a)
    return jnp.concatenate([high, low], 1)


def right_form(b):
    high, low = split(b)
    wide = jnp.concatenate([high, low], 1)
    return jnp.concatenate([wide, wide], 0)


def product(a, b):
    wide = jnp.dot(a, b, preferred_element_type=jnp.float32)
    cols = wide.shape[1] // 2
    return wide[:, :cols] + wide[:, cols:]


def polar_map(crosses):
    order = crosses[0].shape[0]
    row, lane = places((order, order))
    eye = row == lane
    traces = [jnp.sum(jnp.where(eye, c, 0.0), keepdims=True) for c in crosses]
    grams = [c / t for c, t in zip(crosses, traces)]
    maps = [None] * len(crosses)
    for step in range(NS_STEPS):
        factors = [jnp.where(eye, 1.5 - 0.5 * g, -0.5 * g) for g in grams]
        rights = [right_form(m) for m in factors]
        if step < NS_STEPS - 1:
            halves = [product(left_form(g), r) for g, r in zip(grams, rights)]
            grams = [product(left_form(t), r) for t, r in zip(halves, rights)]
        if step == 0:
            maps = factors
        else:
            maps = [product(left_form(q), r) for q, r in zip(maps, rights)]
    return [q * lax.rsqrt(t) for q, t in zip(maps, traces)]


def map_kernel(
    n, spectra, weights, out, held, root, sums_out, sums_in, maps_out, maps_in,
    load_sem, sum_send, sum_recv, map_send, map_recv,
):
    me = lax.axis_index("pts")
    _, group, var_count, points, cols = held.shape
    half = cols // 2
    quarter = half // 2

    def peer(k):
        return lax.rem(me + 1 + k, n)

    def source(k):
        return lax.rem(me + (n - 1) - k, n)

    def load(k):
        return pltpu.make_async_copy(
            spectra.at[pl.ds(peer(k) * group, group)], held.at[k], load_sem.at[k]
        )

    def sum_copy(k):
        return pltpu.make_async_remote_copy(
            src_ref=sums_out.at[k], dst_ref=sums_in.at[k], send_sem=sum_send.at[k],
            recv_sem=sum_recv.at[k], device_id={"pts": peer(k)}, device_id_type=MESH,
        )

    def map_copy(k):
        return pltpu.make_async_remote_copy(
            src_ref=maps_out, dst_ref=maps_in.at[k], send_sem=map_send.at[k],
            recv_sem=map_recv.at[k], device_id={"pts": peer(k)}, device_id_type=MESH,
        )

    barrier = pltpu.get_barrier_semaphore()
    for k in range(n - 1):
        pl.semaphore_signal(barrier, inc=1, device_id={"pts": peer(k)}, device_id_type=MESH)
    load(n - 1).start()
    for k in range(n - 1):
        load(k).start()
    root[...] = jnp.broadcast_to(jnp.sqrt(weights[...]), (cols, points)).T

    def packed_sums(k, j):
        total = jnp.zeros((cols, cols), jnp.float32)
        for v in range(var_count):
            rows = (held[k, j, v].astype(jnp.float32) * root[...]).astype(jnp.bfloat16)
            total = total + lax.dot_general(
                rows, rows, (((0,), (0,)), ((), ())), preferred_element_type=jnp.float32
            )
        top, bottom = total[:half], pltpu.roll(total[half:], half, 1)
        lane = places(top.shape)[1]
        return pack(top + jnp.where(lane < half, bottom, -bottom))

    load(n - 1).wait()
    own = [packed_sums(n - 1, j) for j in range(group)]
    pl.semaphore_wait(barrier, n - 1)

    @pl.loop(0, n - 1)
    def _(k):
        load(k).wait()
        for j in range(group):
            sums_out[k, pl.ds(j * quarter, quarter)] = packed_sums(k, j)
        sum_copy(k).start()

    for k in range(n - 1):
        sum_copy(k).wait_recv()
        for j in range(group):
            own[j] = own[j] + sums_in[k, pl.ds(j * quarter, quarter)]

    maps = polar_map([unpack(o) for o in own])
    for j in range(group):
        maps_out[pl.ds(j * quarter, quarter)] = pack(maps[j][:half])
    for k in range(n - 1):
        map_copy(k).start()
    for j in range(group):
        out[me * group + j] = maps[j].astype(out.dtype)

    @pl.loop(0, n - 1)
    def _(k):
        map_copy(k).wait_recv()
        for j in range(group):
            full = unpack(maps_in[k, pl.ds(j * quarter, quarter)])
            out[source(k) * group + j] = full.astype(out.dtype)

    @pl.loop(0, n - 1)
    def _(k):
        sum_copy(k).wait_send()
        map_copy(k).wait_send()


def shape_kernel(spectra, mapping, out):
    pair, var_count, points, cols = spectra.shape
    if pair == 1:
        right = mapping[0]
    else:
        zero = jnp.zeros((cols, cols), mapping.dtype)
        right = jnp.concatenate(
            [
                jnp.concatenate([mapping[0], zero], 1),
                jnp.concatenate([zero, mapping[1]], 1),
            ],
            0,
        )
    for v in range(var_count):
        left = jnp.concatenate([spectra[f, v] for f in range(pair)], 1)
        result = jnp.dot(left, right, preferred_element_type=jnp.float32).astype(out.dtype)
        for f in range(pair):
            out[f, v] = result[:, f * cols : (f + 1) * cols]


def local(n, spectra, weights):
    freq_count, var_count, points, cols = spectra.shape
    group = freq_count // n
    quarter = cols // 4
    mapping = pl.pallas_call(
        functools.partial(map_kernel, n),
        out_shape=jax.ShapeDtypeStruct((freq_count, cols, cols), jnp.bfloat16),
        in_specs=[
            pl.BlockSpec(memory_space=pl.ANY),
            pl.BlockSpec(memory_space=pltpu.VMEM),
        ],
        out_specs=pl.BlockSpec(memory_space=pltpu.VMEM),
        scratch_shapes=[
            pltpu.VMEM((n, group, var_count, points, cols), jnp.bfloat16),
            pltpu.VMEM((points, cols), jnp.float32),
            pltpu.VMEM((n - 1, group * quarter, cols), jnp.float32),
            pltpu.VMEM((n - 1, group * quarter, cols), jnp.float32),
            pltpu.VMEM((group * quarter, cols), jnp.float32),
            pltpu.VMEM((n - 1, group * quarter, cols), jnp.float32),
            pltpu.SemaphoreType.DMA((n,)),
            pltpu.SemaphoreType.DMA((n - 1,)),
            pltpu.SemaphoreType.DMA((n - 1,)),
            pltpu.SemaphoreType.DMA((n - 1,)),
            pltpu.SemaphoreType.DMA((n - 1,)),
        ],
        compiler_params=pltpu.CompilerParams(
            collective_id=0, has_side_effects=True, vmem_limit_bytes=32 * 1024 * 1024
        ),
        name="polar_mapping",
    )(spectra, weights.reshape(1, points))
    pair = 2 if freq_count % 2 == 0 else 1
    block = pl.BlockSpec((pair, var_count, points, cols), lambda f: (f, 0, 0, 0))
    return pl.pallas_call(
        shape_kernel,
        grid=(freq_count // pair,),
        out_shape=jax.ShapeDtypeStruct(spectra.shape, jnp.bfloat16),
        in_specs=[block, pl.BlockSpec((pair, cols, cols), lambda f: (f, 0, 0))],
        out_specs=block,
        compiler_params=pltpu.CompilerParams(vmem_limit_bytes=32 * 1024 * 1024),
        name="mode_shapes",
    )(spectra, mapping)


def solution(mesh):
    in_specs = (P("freq", None, "pts", None), P("pts"))
    out_specs = P("freq", None, "pts", None)
    return jax.shard_map(
        functools.partial(local, mesh.shape["pts"]),
        mesh=mesh, in_specs=in_specs, out_specs=out_specs, check_vma=False,
    )
```

time: 518 us -> 32.7 us (0.06)
  other arithmetic: 243 us -> 0 us
  matrix products: 160 us -> 0 us
  waiting for transfers between devices: 75.2 us -> 0 us
  Pallas kernels: 0 us -> 29.4 us
  between operations: 14 us -> 0.01 us
  loops' own time: 10.3 us -> 0 us
  local copies, waits for them, and re-layouts: 10.8 us -> 3.16 us
    dot_general x150 -> x0, matrix products: 160 us -> none  [the longest x128 120 us: back_step(): jnp.einsum('fj,fjk->fk', factor_row, solved, precision=lax.Precision.HIGH...]
    add x256 -> x0, other arithmetic: 108 us -> none  [the longest x128 82.9 us: eliminate(): factor = factor + scaled[:, None, :] * picker[None, :, None]]
    reduce_sum x513 -> x0, other arithmetic: 107 us -> none  [the longest x128 44 us: eliminate(): current = jnp.sum(working * picker[None, None, :], axis=2) * below[None, :]]
    psum x1 -> x0, waiting for transfers between devices: 75.1 us -> none  [local(): summed = lax.psum(packed, 'pts')]
    pallas_call x0 -> x2, Pallas kernels: none -> 29.4 us  [the longest x1 24.3 us: local(): pl.pallas_call(functools.partial(map_kernel, n), out_shape=jax.ShapeDtype...]
    div x256 -> x0, other arithmetic: 20.1 us -> none  [the longest x128 10.1 us: eliminate(): scaled = current / pivot[:, None]]
    another operation x2 -> x0, loops' own time: 10.3 us -> none  [the longest x1 5.43 us: upper_of(): working, factor = lax.fori_loop(0, order, eliminate, start)]
    convert_element_type x1 -> x0, local copies, waits for them, and re-layouts: 7.83 us -> none  [local(): return shapes.astype(jnp.bfloat16)]
  transfers between devices with their start and end apart: 1 -> 0, of which waited for: 1 -> 0; matrix products, arithmetic and copies ran while one was open for 0% -> 0% of each run, Pallas kernels for 0% -> 0%
where the time goes in v1:
time: 32.7 us; the launch traced here: 32.6 us
  Pallas kernels  29.4 us (90%)
  local copies, waits for them, and re-layouts  3.16 us (10%)
    pallas_call x1, Pallas kernels, local(): pl.pallas_call(functools.partial(map_kernel, n), out_shape=jax.ShapeDtype...  24.3 us
    pallas_call x1, Pallas kernels, local(): pl.pallas_call(shape_kernel, grid=(freq_count // pair,), out_shape=jax.Sh...  5.1 us
    unnamed x4, local copies, waits for them, and re-layouts  3.16 us

profile of v1, /device:TPU:0, one launch (start us, length us, event | category | flops | bytes accessed | tf_op | source)
XLA Modules:
  0.0 32.6 jit_solution(12112234815545305426)
XLA Ops:
  0.0 0.0 copy-start
  0.0 2.5 %copy-done = bf16[16,5,256,128]{3,2,1,0:T(8,128)(2,1)S(1)} copy-done((bf16[16,5,256,128]{3,2,1,0:T(8,128)(2,1)S(1)}, bf16[16,5,256,128]{3,2,1,0:T(8,128)(2,1)}, u32[]{:S(2)}) %copy-start) | copy-done | bytes 5242904
  2.5 0.0 copy-start.1
  2.5 0.7 %copy-done.1 = f32[256]{0:T(256)S(1)} copy-done((f32[256]{0:T(256)S(1)}, f32[256]{0:T(256)}, u32[]{:S(2)}) %copy-start.1) | copy-done | bytes 1048
  3.2 24.3 %polar_mapping.1.mapping = bf16[16,128,128]{2,1,0:T(8,128)(2,1)S(1)} custom-call(bf16[16,5,256,128]{3,2,1,0:T(8,128)(2,1)S(1)} %copy-done, f32[1,256]{1,0:T(1,128)S(1)} %bitcast.1), custom_call_target="tpu_custom_call" | custom-call | tf_op jit(solution)/shard_map/polar_mapping/pallas_call | solution.py:206
  27.5 5.1 %mode_shapes.1 = bf16[16,5,256,128]{3,2,1,0:T(8,128)(2,1)} custom-call(bf16[16,5,256,128]{3,2,1,0:T(8,128)(2,1)S(1)} %copy-done, bf16[16,128,128]{2,1,0:T(8,128)(2,1)S(1)} %polar_mapping.1.mapping), custom_call_target="tpu_custom_call" | custom-call | tf_op jit(solution)/shard_map/mode_shapes/pallas_call | solution.py:234
Async XLA Ops:
  0.0 2.5 %copy-start = (bf16[16,5,256,128]{3,2,1,0:T(8,128)(2,1)S(1)}, bf16[16,5,256,128]{3,2,1,0:T(8,128)(2,1)}, u32[]{:S(2)}) copy-start(bf16[16,5,256,128]{3,2,1,0:T(8,128)(2,1)} %spectra.3) | copy-start | bytes 15728644
  2.5 0.7 %copy-start.1 = (f32[256]{0:T(256)S(1)}, f32[256]{0:T(256)}, u32[]{:S(2)}) copy-start(f32[256]{0:T(256)} %param.3) | copy-start | bytes 3076

commit v2 on v1

v2 whole, which is shorter than its diff:
```python
import functools

import jax
import jax.numpy as jnp
from jax import lax
from jax.experimental import pallas as pl
from jax.experimental.pallas import tpu as pltpu
from jax.sharding import PartitionSpec as P

NS_STEPS = 10
MESH = pl.DeviceIdType.MESH


def places(shape):
    return (
        lax.broadcasted_iota(jnp.int32, shape, 0),
        lax.broadcasted_iota(jnp.int32, shape, 1),
    )


def pack(top):
    half, cols = top.shape
    row, lane = places(top.shape)
    left = lane < half
    upper = jnp.where(left, lane, lane - half) >= row
    rolled = pltpu.roll(top, half, 1)
    both = jnp.where(jnp.logical_xor(left, upper), rolled, top)
    quarter = half // 2
    return jnp.where(left[:quarter], both[:quarter], both[quarter:])


def unpack(packed):
    quarter, cols = packed.shape
    half = 2 * quarter
    left = places(packed.shape)[1] < half
    rolled = pltpu.roll(packed, half, 1)
    top = jnp.where(left, packed, rolled)
    bottom = jnp.where(left, rolled, packed)
    full = jnp.concatenate([top, bottom, top, bottom], 0)
    flipped = full.T
    row, lane = places(full.shape)
    row_left, lane_left = row < half, lane < half
    i = jnp.where(row_left, row, row - half)
    j = jnp.where(lane_left, lane, lane - half)
    real = jnp.where(j >= i, full, flipped)
    imag = jnp.where(j < i, full, jnp.where(j > i, -flipped, 0.0))
    imag = jnp.where(row_left, imag, -imag)
    return jnp.where(jnp.logical_xor(row_left, lane_left), imag, real)


def split(a):
    high = a.astype(jnp.bfloat16)
    low = (a - high.astype(jnp.float32)).astype(jnp.bfloat16)
    return high, low


def left_form(a):
    return jnp.concatenate(split(a), 1)


def product(left, right):
    wide = jnp.dot(left, right, preferred_element_type=jnp.float32)
    cols = wide.shape[1] // 2
    return wide[:, :cols] + wide[:, cols:]


def polar_map(crosses):
    order = crosses[0].shape[0]
    row, lane = places((order, order))
    eye = row == lane
    traces = [jnp.sum(jnp.where(eye, c, 0.0), keepdims=True) for c in crosses]
    grams = [c / t for c, t in zip(crosses, traces)]
    maps = [jnp.where(eye, 1.5 - 0.5 * g, -0.5 * g) for g in grams]
    for step in range(NS_STEPS):
        lefts = [left_form(g) for g in grams]
        rights = [jnp.concatenate([g, g], 0) for g in lefts]
        if step == 0:
            squares = [product(g, r) for g, r in zip(lefts, rights)]
        elif step < NS_STEPS - 1:
            both = [
                product(jnp.concatenate([g, left_form(q)], 0), r)
                for g, q, r in zip(lefts, maps, rights)
            ]
            squares = [x[:order] for x in both]
            maps = [1.5 * q - 0.5 * x[order:] for q, x in zip(maps, both)]
        else:
            maps = [1.5 * q - 0.5 * product(left_form(q), r) for q, r in zip(maps, rights)]
        if step < NS_STEPS - 1:
            halves = [1.5 * g - 0.5 * x for g, x in zip(grams, squares)]
            grams = [
                1.5 * t - 0.5 * product(left_form(t), r) for t, r in zip(halves, rights)
            ]
    return [q * lax.rsqrt(t) for q, t in zip(maps, traces)]


def main_kernel(
    n, spectra, weights, out, held, row_weights, root, pair_out, pair_in, sums_out, sums_in,
    maps_out, maps_in, maps_pair, load_sem, weight_sem, pair_send, pair_recv, sum_send, sum_recv,
    map_send, map_recv, fwd_send, fwd_recv,
):
    major = n // 2
    me = lax.axis_index("pts")
    a, b = me // 2, lax.rem(me, 2)
    other = 1 - b
    partner = a * 2 + other
    _, var_count, points, cols = held.shape
    group = held.shape[0] // n
    half = cols // 2
    quarter = half // 2

    def ahead(d):
        return lax.rem(a + d, major)

    def behind(d):
        return lax.rem(a + major - d, major)

    def load(d, side):
        start = (ahead(d) * 2 + (b if side == 0 else other)) * group
        rows = pl.ds(start, group)
        return pltpu.make_async_copy(spectra.at[rows], held.at[rows], load_sem.at[side, d])

    def send(src, dst, send_sem, recv_sem, target):
        return pltpu.make_async_remote_copy(
            src_ref=src, dst_ref=dst, send_sem=send_sem, recv_sem=recv_sem,
            device_id={"pts": target}, device_id_type=MESH,
        )

    def pair_copy(d):
        return send(pair_out.at[d], pair_in.at[d], pair_send.at[d], pair_recv.at[d], partner)

    def sum_copy(d):
        return send(
            sums_out.at[d - 1], sums_in.at[d - 1], sum_send.at[d - 1], sum_recv.at[d - 1],
            ahead(d) * 2 + b,
        )

    def map_copy(d):
        return send(
            maps_out, maps_in.at[d - 1], map_send.at[d - 1], map_recv.at[d - 1], ahead(d) * 2 + b
        )

    def fwd_copy(d):
        src = maps_out if isinstance(d, int) and d == 0 else maps_in.at[d - 1]
        return send(src, maps_pair.at[d], fwd_send.at[d], fwd_recv.at[d], partner)

    barrier = pltpu.get_barrier_semaphore()
    pl.semaphore_signal(barrier, inc=1, device_id={"pts": partner}, device_id_type=MESH)
    for d in range(1, major):
        pl.semaphore_signal(
            barrier, inc=1, device_id={"pts": ahead(d) * 2 + b}, device_id_type=MESH
        )
    weight_copy = pltpu.make_async_copy(weights, row_weights, weight_sem)
    weight_copy.start()
    load(0, 0).start()
    for side in (1, 0):
        for d in range(1, major):
            load(d, side).start()
        if side == 1:
            load(0, 1).start()
    weight_copy.wait()
    root[...] = jnp.broadcast_to(jnp.sqrt(row_weights[...]), (cols, points)).T

    def packed_sums(freq):
        total = jnp.zeros((cols, cols), jnp.float32)
        for v in range(var_count):
            rows = (held[freq, v].astype(jnp.float32) * root[...]).astype(jnp.bfloat16)
            total = total + lax.dot_general(
                rows, rows, (((0,), (0,)), ((), ())), preferred_element_type=jnp.float32
            )
        top, bottom = total[:half], pltpu.roll(total[half:], half, 1)
        lane = places(top.shape)[1]
        return pack(top + jnp.where(lane < half, bottom, -bottom))

    def part(j):
        return pl.ds(j * quarter, quarter)

    def apply(owner, maps):
        first = owner * group
        if group == 2:
            zero = jnp.zeros((cols, cols), jnp.bfloat16)
            right = jnp.concatenate(
                [
                    jnp.concatenate([maps[0], zero], 1),
                    jnp.concatenate([zero, maps[1]], 1),
                ],
                0,
            )
            for v in range(var_count):
                left = jnp.concatenate([held[first, v], held[first + 1, v]], 1)
                wide = jnp.dot(left, right, preferred_element_type=jnp.float32)
                wide = wide.astype(out.dtype)
                out[first, v] = wide[:, :cols]
                out[first + 1, v] = wide[:, cols:]
        else:
            for j in range(group):
                for v in range(var_count):
                    out[first + j, v] = jnp.dot(
                        held[first + j, v], maps[j], preferred_element_type=jnp.float32
                    ).astype(out.dtype)

    load(0, 0).wait()
    own = [packed_sums(me * group + j) for j in range(group)]
    pl.semaphore_wait(barrier, major)

    @pl.loop(0, major)
    def _(i):
        d = lax.rem(i + 1, major)
        load(d, 1).wait()
        for j in range(group):
            pair_out[d, part(j)] = packed_sums((ahead(d) * 2 + other) * group + j)
        pair_copy(d).start()

    @pl.loop(1, major)
    def _(d):
        load(d, 0).wait()
        sums = [packed_sums((ahead(d) * 2 + b) * group + j) for j in range(group)]
        pair_copy(d).wait_recv()
        for j in range(group):
            sums_out[d - 1, part(j)] = sums[j] + pair_in[d, part(j)]
        sum_copy(d).start()

    pair_copy(0).wait_recv()
    for j in range(group):
        own[j] = own[j] + pair_in[0, part(j)]
    for d in range(1, major):
        sum_copy(d).wait_recv()
        for j in range(group):
            own[j] = own[j] + sums_in[d - 1, part(j)]

    maps = polar_map([unpack(o) for o in own])
    for j in range(group):
        maps_out[part(j)] = pack(maps[j][:half])
    for d in range(1, major):
        map_copy(d).start()
    fwd_copy(0).start()
    apply(me, [m.astype(jnp.bfloat16) for m in maps])

    @pl.loop(1, major)
    def _(d):
        map_copy(d).wait_recv()
        fwd_copy(d).start()
        apply(
            behind(d) * 2 + b,
            [unpack(maps_in[d - 1, part(j)]).astype(jnp.bfloat16) for j in range(group)],
        )

    @pl.loop(0, major)
    def _(d):
        send(maps_out, maps_pair.at[d], fwd_send.at[d], fwd_recv.at[d], partner).wait_recv()
        apply(
            behind(d) * 2 + other,
            [unpack(maps_pair[d, part(j)]).astype(jnp.bfloat16) for j in range(group)],
        )

    for d in range(major):
        pair_copy(d).wait_send()
        fwd_copy(d).wait_send()
        if d > 0:
            sum_copy(d).wait_send()
            map_copy(d).wait_send()


def store_kernel(shapes, out, sems):
    copies = [
        pltpu.make_async_copy(shapes.at[f], out.at[f], sems.at[f]) for f in range(shapes.shape[0])
    ]
    for copy in copies:
        copy.start()
    for copy in copies:
        copy.wait()


def local(n, spectra, weights):
    freq_count, var_count, points, cols = spectra.shape
    block = (freq_count // n * (cols // 4), cols)
    major = n // 2
    dma = pltpu.SemaphoreType.DMA
    shapes = pl.pallas_call(
        functools.partial(main_kernel, n),
        out_shape=jax.ShapeDtypeStruct(spectra.shape, jnp.bfloat16),
        in_specs=[pl.BlockSpec(memory_space=pltpu.HBM)] * 2,
        out_specs=pl.BlockSpec(memory_space=pltpu.VMEM),
        scratch_shapes=[
            pltpu.VMEM(spectra.shape, jnp.bfloat16),
            pltpu.VMEM((1, points), jnp.float32),
            pltpu.VMEM((points, cols), jnp.float32),
            pltpu.VMEM((major, *block), jnp.float32),
            pltpu.VMEM((major, *block), jnp.float32),
            pltpu.VMEM((major - 1, *block), jnp.float32),
            pltpu.VMEM((major - 1, *block), jnp.float32),
            pltpu.VMEM(block, jnp.float32),
            pltpu.VMEM((major - 1, *block), jnp.float32),
            pltpu.VMEM((major, *block), jnp.float32),
            dma((2, major)),
            dma,
            dma((major,)),
            dma((major,)),
            dma((major - 1,)),
            dma((major - 1,)),
            dma((major - 1,)),
            dma((major - 1,)),
            dma((major,)),
            dma((major,)),
        ],
        compiler_params=pltpu.CompilerParams(
            collective_id=0, has_side_effects=True, vmem_limit_bytes=32 * 1024 * 1024
        ),
        name="polar_shapes",
    )(
        pltpu.with_memory_space_constraint(spectra, pltpu.HBM),
        pltpu.with_memory_space_constraint(weights.reshape(1, points), pltpu.HBM),
    )
    return pl.pallas_call(
        store_kernel,
        out_shape=jax.ShapeDtypeStruct(spectra.shape, jnp.bfloat16),
        in_specs=[pl.BlockSpec(memory_space=pltpu.VMEM)],
        out_specs=pl.BlockSpec(memory_space=pltpu.HBM),
        scratch_shapes=[dma((freq_count,))],
        compiler_params=pltpu.CompilerParams(vmem_limit_bytes=32 * 1024 * 1024),
        name="store_shapes",
    )(shapes)


def solution(mesh):
    in_specs = (P("freq", None, "pts", None), P("pts"))
    out_specs = P("freq", None, "pts", None)
    return jax.shard_map(
        functools.partial(local, mesh.shape["pts"]),
        mesh=mesh, in_specs=in_specs, out_specs=out_specs, check_vma=False,
    )
```

time: 32.7 us -> 28.3 us (0.87)
  local copies, waits for them, and re-layouts: 3.16 us -> 0 us
  Pallas kernels: 29.4 us -> 28.2 us
    unnamed x4 -> x0, local copies, waits for them, and re-layouts: 3.16 us -> none
    pallas_call x2, Pallas kernels: 29.4 us -> 28.2 us  [the longest x1 25.7 us: local(): pl.pallas_call(functools.partial(main_kernel, n), out_shape=jax.ShapeDtyp...]
where the time goes in v2:
time: 28.3 us; the launch traced here: 28.2 us
  Pallas kernels  28.2 us (100%)
    pallas_call x1, Pallas kernels, local(): pl.pallas_call(functools.partial(main_kernel, n), out_shape=jax.ShapeDtyp...  25.7 us
    pallas_call x1, Pallas kernels, local(): pl.pallas_call(store_kernel, out_shape=jax.ShapeDtypeStruct(spectra.shape...  2.46 us

profile of v2, /device:TPU:0, one launch (start us, length us, event | category | flops | bytes accessed | tf_op | source)
XLA Modules:
  0.0 28.2 jit_solution(14476329707195743311)
XLA Ops:
  0.0 25.7 %polar_shapes.1.shapes = bf16[16,5,256,128]{3,2,1,0:T(8,128)(2,1)S(1)} custom-call(bf16[16,5,256,128]{3,2,1,0:T(8,128)(2,1)} %spectra.1, f32[1,256]{1,0:T(1,128)} %bitcast.1), custom_call_target="tpu_custom_call" | custom-call | tf_op jit(solution)/shard_map/polar_shapes/pallas_call | solution.py:278
  25.7 2.5 %store_shapes.1 = bf16[16,5,256,128]{3,2,1,0:T(8,128)(2,1)} custom-call(bf16[16,5,256,128]{3,2,1,0:T(8,128)(2,1)S(1)} %polar_shapes.1.shapes), custom_call_target="tpu_custom_call" | custom-call | tf_op jit(solution)/shard_map/store_shapes/pallas_call | solution.py:313

commit v3 on v2

--- a/solution.py
+++ b/solution.py
@@ -93,9 +93,35 @@
     return [q * lax.rsqrt(t) for q, t in zip(maps, traces)]
 
 
+def apply(held, first, maps, out, place):
+    group = len(maps)
+    _, var_count, points, cols = held.shape
+    maps = [m.astype(jnp.bfloat16) for m in maps]
+    if group == 2:
+        zero = jnp.zeros((cols, cols), jnp.bfloat16)
+        right = jnp.concatenate(
+            [
+                jnp.concatenate([maps[0], zero], 1),
+                jnp.concatenate([zero, maps[1]], 1),
+            ],
+            0,
+        )
+        for v in range(var_count):
+            left = jnp.concatenate([held[first, v], held[first + 1, v]], 1)
+            wide = jnp.dot(left, right, preferred_element_type=jnp.float32).astype(out.dtype)
+            out[place, v] = wide[:, :cols]
+            out[place + 1, v] = wide[:, cols:]
+    else:
+        for j in range(group):
+            for v in range(var_count):
+                out[place + j, v] = jnp.dot(
+                    held[first + j, v], maps[j], preferred_element_type=jnp.float32
+                ).astype(out.dtype)
+
+
 def main_kernel(
-    n, spectra, weights, out, held, row_weights, root, pair_out, pair_in, sums_out, sums_in,
-    maps_out, maps_in, maps_pair, load_sem, weight_sem, pair_send, pair_recv, sum_send, sum_recv,
+    n, spectra, weights, out, held, maps_pair, row_weights, root, pair_out, pair_in, sums_out,
+    sums_in, maps_out, maps_in, load_sem, weight_sem, pair_send, pair_recv, sum_send, sum_recv,
     map_send, map_recv, fwd_send, fwd_recv,
 ):
     major = n // 2
@@ -151,22 +177,18 @@
         )
     weight_copy = pltpu.make_async_copy(weights, row_weights, weight_sem)
     weight_copy.start()
-    load(0, 0).start()
     for side in (1, 0):
-        for d in range(1, major):
-            load(d, side).start()
-        if side == 1:
-            load(0, 1).start()
+        for d in range(1, major + 1):
+            load(d % major, side).start()
     weight_copy.wait()
     root[...] = jnp.broadcast_to(jnp.sqrt(row_weights[...]), (cols, points)).T
 
     def packed_sums(freq):
-        total = jnp.zeros((cols, cols), jnp.float32)
-        for v in range(var_count):
-            rows = (held[freq, v].astype(jnp.float32) * root[...]).astype(jnp.bfloat16)
-            total = total + lax.dot_general(
-                rows, rows, (((0,), (0,)), ((), ())), preferred_element_type=jnp.float32
-            )
+        rows = (held[freq].astype(jnp.float32) * root[...]).astype(jnp.bfloat16)
+        rows = rows.reshape(var_count * points, cols)
+        total = lax.dot_general(
+            rows, rows, (((0,), (0,)), ((), ())), preferred_element_type=jnp.float32
+        )
         top, bottom = total[:half], pltpu.roll(total[half:], half, 1)
         lane = places(top.shape)[1]
         return pack(top + jnp.where(lane < half, bottom, -bottom))
@@ -174,40 +196,25 @@
     def part(j):
         return pl.ds(j * quarter, quarter)
 
-    def apply(owner, maps):
-        first = owner * group
-        if group == 2:
-            zero = jnp.zeros((cols, cols), jnp.bfloat16)
-            right = jnp.concatenate(
-                [
-                    jnp.concatenate([maps[0], zero], 1),
-                    jnp.concatenate([zero, maps[1]], 1),
-                ],
-                0,
-            )
-            for v in range(var_count):
-                left = jnp.concatenate([held[first, v], held[first + 1, v]], 1)
-                wide = jnp.dot(left, right, preferred_element_type=jnp.float32)
-                wide = wide.astype(out.dtype)
-                out[first, v] = wide[:, :cols]
-                out[first + 1, v] = wide[:, cols:]
-        else:
-            for j in range(group):
-                for v in range(var_count):
-                    out[first + j, v] = jnp.dot(
-                        held[first + j, v], maps[j], preferred_element_type=jnp.float32
-                    ).astype(out.dtype)
-
-    load(0, 0).wait()
-    own = [packed_sums(me * group + j) for j in range(group)]
-    pl.semaphore_wait(barrier, major)
-
-    @pl.loop(0, major)
-    def _(i):
-        d = lax.rem(i + 1, major)
+    def pair_sums(d):
         load(d, 1).wait()
         for j in range(group):
             pair_out[d, part(j)] = packed_sums((ahead(d) * 2 + other) * group + j)
+
+    early = min(2, major)
+
+    @pl.loop(0, early)
+    def _(i):
+        pair_sums(lax.rem(i + 1, major))
+
+    pl.semaphore_wait(barrier, major)
+    for i in range(early):
+        pair_copy((i + 1) % major).start()
+
+    @pl.loop(early, major)
+    def _(i):
+        d = lax.rem(i + 1, major)
+        pair_sums(d)
         pair_copy(d).start()
 
     @pl.loop(1, major)
@@ -219,6 +226,8 @@
             sums_out[d - 1, part(j)] = sums[j] + pair_in[d, part(j)]
         sum_copy(d).start()
 
+    load(0, 0).wait()
+    own = [packed_sums(me * group + j) for j in range(group)]
     pair_copy(0).wait_recv()
     for j in range(group):
         own[j] = own[j] + pair_in[0, part(j)]
@@ -233,24 +242,18 @@
     for d in range(1, major):
         map_copy(d).start()
     fwd_copy(0).start()
-    apply(me, [m.astype(jnp.bfloat16) for m in maps])
+    apply(held, me * group, maps, out, me * group)
 
     @pl.loop(1, major)
     def _(d):
         map_copy(d).wait_recv()
         fwd_copy(d).start()
-        apply(
-            behind(d) * 2 + b,
-            [unpack(maps_in[d - 1, part(j)]).astype(jnp.bfloat16) for j in range(group)],
-        )
+        first = (behind(d) * 2 + b) * group
+        apply(held, first, [unpack(maps_in[d - 1, part(j)]) for j in range(group)], out, first)
 
     @pl.loop(0, major)
     def _(d):
         send(maps_out, maps_pair.at[d], fwd_send.at[d], fwd_recv.at[d], partner).wait_recv()
-        apply(
-            behind(d) * 2 + other,
-            [unpack(maps_pair[d, part(j)]).astype(jnp.bfloat16) for j in range(group)],
-        )
 
     for d in range(major):
         pair_copy(d).wait_send()
@@ -260,14 +263,39 @@
             map_copy(d).wait_send()
 
 
-def store_kernel(shapes, out, sems):
-    copies = [
-        pltpu.make_async_copy(shapes.at[f], out.at[f], sems.at[f]) for f in range(shapes.shape[0])
-    ]
-    for copy in copies:
-        copy.start()
-    for copy in copies:
-        copy.wait()
+def finish_kernel(n, shapes, held, maps_pair, out, late, early_sem, late_sem):
+    major = n // 2
+    me = lax.axis_index("pts")
+    a, b = me // 2, lax.rem(me, 2)
+    group = held.shape[0] // n
+    quarter = maps_pair.shape[1] // group
+
+    def early_copy(d):
+        rows = pl.ds((lax.rem(a + major - d, major) * 2 + b) * group, group)
+        return pltpu.make_async_copy(shapes.at[rows], out.at[rows], early_sem.at[d])
+
+    def late_first(d):
+        return (lax.rem(a + major - d, major) * 2 + 1 - b) * group
+
+    def late_copy(d):
+        return pltpu.make_async_copy(
+            late.at[pl.ds(d * group, group)],
+            out.at[pl.ds(late_first(d), group)],
+            late_sem.at[d],
+        )
+
+    for d in range(major):
+        early_copy(d).start()
+
+    @pl.loop(0, major)
+    def _(d):
+        maps = [unpack(maps_pair[d, pl.ds(j * quarter, quarter)]) for j in range(group)]
+        apply(held, late_first(d), maps, late, d * group)
+        late_copy(d).start()
+
+    for d in range(major):
+        early_copy(d).wait()
+        late_copy(d).wait()
 
 
 def local(n, spectra, weights):
@@ -275,13 +303,16 @@
     block = (freq_count // n * (cols // 4), cols)
     major = n // 2
     dma = pltpu.SemaphoreType.DMA
-    shapes = pl.pallas_call(
+    shapes, held, maps_pair = pl.pallas_call(
         functools.partial(main_kernel, n),
-        out_shape=jax.ShapeDtypeStruct(spectra.shape, jnp.bfloat16),
+        out_shape=[
+            jax.ShapeDtypeStruct(spectra.shape, jnp.bfloat16),
+            jax.ShapeDtypeStruct(spectra.shape, jnp.bfloat16),
+            jax.ShapeDtypeStruct((major, *block), jnp.float32),
+        ],
         in_specs=[pl.BlockSpec(memory_space=pltpu.HBM)] * 2,
-        out_specs=pl.BlockSpec(memory_space=pltpu.VMEM),
+        out_specs=[pl.BlockSpec(memory_space=pltpu.VMEM)] * 3,
         scratch_shapes=[
-            pltpu.VMEM(spectra.shape, jnp.bfloat16),
             pltpu.VMEM((1, points), jnp.float32),
             pltpu.VMEM((points, cols), jnp.float32),
             pltpu.VMEM((major, *block), jnp.float32),
@@ -290,7 +321,6 @@
             pltpu.VMEM((major - 1, *block), jnp.float32),
             pltpu.VMEM(block, jnp.float32),
             pltpu.VMEM((major - 1, *block), jnp.float32),
-            pltpu.VMEM((major, *block), jnp.float32),
             dma((2, major)),
             dma,
             dma((major,)),
@@ -311,14 +341,18 @@
         pltpu.with_memory_space_constraint(weights.reshape(1, points), pltpu.HBM),
     )
     return pl.pallas_call(
-        store_kernel,
+        functools.partial(finish_kernel, n),
         out_shape=jax.ShapeDtypeStruct(spectra.shape, jnp.bfloat16),
-        in_specs=[pl.BlockSpec(memory_space=pltpu.VMEM)],
+        in_specs=[pl.BlockSpec(memory_space=pltpu.VMEM)] * 3,
         out_specs=pl.BlockSpec(memory_space=pltpu.HBM),
-        scratch_shapes=[dma((freq_count,))],
+        scratch_shapes=[
+            pltpu.VMEM((freq_count // 2, *spectra.shape[1:]), jnp.bfloat16),
+            dma((major,)),
+            dma((major,)),
+        ],
         compiler_params=pltpu.CompilerParams(vmem_limit_bytes=32 * 1024 * 1024),
-        name="store_shapes",
-    )(shapes)
+        name="finish_shapes",
+    )(shapes, held, maps_pair)
 
 
 def solution(mesh):

time: 28.3 us -> 27.8 us (0.982)
  Pallas kernels: 28.2 us -> 27.7 us
    pallas_call x2, Pallas kernels: 28.2 us -> 27.7 us  [the longest x1 24.7 us: local(): pl.pallas_call(functools.partial(main_kernel, n), out_shape=[jax.ShapeDty...]
where the time goes in v3:
time: 27.8 us; the launch traced here: 27.7 us
  Pallas kernels  27.7 us (100%)
    pallas_call x1, Pallas kernels, local(): pl.pallas_call(functools.partial(main_kernel, n), out_shape=[jax.ShapeDty...  24.7 us
    pallas_call x1, Pallas kernels, local(): pl.pallas_call(functools.partial(finish_kernel, n), out_shape=jax.ShapeDt...  2.93 us

profile of v3, /device:TPU:0, one launch (start us, length us, event | category | flops | bytes accessed | tf_op | source)
XLA Modules:
  0.0 27.7 jit_solution(14636507668768402637)
XLA Ops:
  0.0 24.7 %polar_shapes.1 = (bf16[16,5,256,128]{3,2,1,0:T(8,128)(2,1)S(1)}, bf16[16,5,256,128]{3,2,1,0:T(8,128)(2,1)S(1)}, f32[4,64,128]{2,1,0:T(8,128)S(1)}) custom-call(bf16[16,5,256,128]{3,2,1,0:T(8,128)(2,1)} %spectra.1, f32[1,256]{1,0:T(1,128)} %bitcast.1), custom_call_target="tpu_custom_call" | custom-call | tf_op jit(solution)/shard_map/polar_shapes/pallas_call | solution.py:306
  24.7 2.9 %finish_shapes.1 = bf16[16,5,256,128]{3,2,1,0:T(8,128)(2,1)} custom-call(bf16[16,5,256,128]{3,2,1,0:T(8,128)(2,1)S(1)} %get-tuple-element.8.shapes, bf16[16,5,256,128]{3,2,1,0:T(8,128)(2,1)S(1)} %get-tuple-element.9.held, f32[4,64,128]{2,1,0:T(8,128)S(1)} %get-tuple-element.10.maps_pair), custom_call_target="tpu_custom_call" | custom-call | tf_op jit(solution)/shard_map/finish_shapes/pallas_call | solution.py:343

commit v4 on v3

--- a/solution.py
+++ b/solution.py
@@ -165,9 +165,12 @@
             maps_out, maps_in.at[d - 1], map_send.at[d - 1], map_recv.at[d - 1], ahead(d) * 2 + b
         )
 
-    def fwd_copy(d):
-        src = maps_out if isinstance(d, int) and d == 0 else maps_in.at[d - 1]
-        return send(src, maps_pair.at[d], fwd_send.at[d], fwd_recv.at[d], partner)
+    via = major // 2
+
+    def cross_copy(d):
+        src = maps_in.at[d - 1] if d == via and d > 0 else maps_out
+        target = partner if d == via else ahead(d) * 2 + other
+        return send(src, maps_pair.at[d], fwd_send.at[d], fwd_recv.at[d], target)
 
     barrier = pltpu.get_barrier_semaphore()
     pl.semaphore_signal(barrier, inc=1, device_id={"pts": partner}, device_id_type=MESH)
@@ -175,6 +178,11 @@
         pl.semaphore_signal(
             barrier, inc=1, device_id={"pts": ahead(d) * 2 + b}, device_id_type=MESH
         )
+    for d in range(1, major):
+        if d != via:
+            pl.semaphore_signal(
+                barrier, inc=1, device_id={"pts": ahead(d) * 2 + other}, device_id_type=MESH
+            )
     weight_copy = pltpu.make_async_copy(weights, row_weights, weight_sem)
     weight_copy.start()
     for side in (1, 0):
@@ -183,23 +191,39 @@
     weight_copy.wait()
     root[...] = jnp.broadcast_to(jnp.sqrt(row_weights[...]), (cols, points)).T
 
-    def packed_sums(freq):
-        rows = (held[freq].astype(jnp.float32) * root[...]).astype(jnp.bfloat16)
-        rows = rows.reshape(var_count * points, cols)
-        total = lax.dot_general(
-            rows, rows, (((0,), (0,)), ((), ())), preferred_element_type=jnp.float32
-        )
+    def fold(total):
         top, bottom = total[:half], pltpu.roll(total[half:], half, 1)
         lane = places(top.shape)[1]
         return pack(top + jnp.where(lane < half, bottom, -bottom))
 
+    def packed_sums(first):
+        sums = []
+        for start in range(0, group, 2):
+            count = min(2, group - start)
+            rows = jnp.concatenate(
+                [
+                    (held[first + start + j].astype(jnp.float32) * root[...])
+                    .astype(jnp.bfloat16)
+                    .reshape(var_count * points, cols)
+                    for j in range(count)
+                ],
+                1,
+            )
+            total = lax.dot_general(
+                rows, rows, (((0,), (0,)), ((), ())), preferred_element_type=jnp.float32
+            )
+            for j in range(count):
+                own_cols = slice(j * cols, (j + 1) * cols)
+                sums.append(fold(total[own_cols, own_cols]))
+        return sums
+
     def part(j):
         return pl.ds(j * quarter, quarter)
 
     def pair_sums(d):
         load(d, 1).wait()
-        for j in range(group):
-            pair_out[d, part(j)] = packed_sums((ahead(d) * 2 + other) * group + j)
+        for j, packed in enumerate(packed_sums((ahead(d) * 2 + other) * group)):
+            pair_out[d, part(j)] = packed
 
     early = min(2, major)
 
@@ -207,7 +231,7 @@
     def _(i):
         pair_sums(lax.rem(i + 1, major))
 
-    pl.semaphore_wait(barrier, major)
+    pl.semaphore_wait(barrier, major + max(major - 2, 0))
     for i in range(early):
         pair_copy((i + 1) % major).start()
 
@@ -220,14 +244,14 @@
     @pl.loop(1, major)
     def _(d):
         load(d, 0).wait()
-        sums = [packed_sums((ahead(d) * 2 + b) * group + j) for j in range(group)]
+        sums = packed_sums((ahead(d) * 2 + b) * group)
         pair_copy(d).wait_recv()
         for j in range(group):
             sums_out[d - 1, part(j)] = sums[j] + pair_in[d, part(j)]
         sum_copy(d).start()
 
     load(0, 0).wait()
-    own = [packed_sums(me * group + j) for j in range(group)]
+    own = packed_sums(me * group)
     pair_copy(0).wait_recv()
     for j in range(group):
         own[j] = own[j] + pair_in[0, part(j)]
@@ -239,25 +263,35 @@
     maps = polar_map([unpack(o) for o in own])
     for j in range(group):
         maps_out[part(j)] = pack(maps[j][:half])
-    for d in range(1, major):
-        map_copy(d).start()
-    fwd_copy(0).start()
-    apply(held, me * group, maps, out, me * group)
-
-    @pl.loop(1, major)
-    def _(d):
-        map_copy(d).wait_recv()
-        fwd_copy(d).start()
+    def take(d):
         first = (behind(d) * 2 + b) * group
         apply(held, first, [unpack(maps_in[d - 1, part(j)]) for j in range(group)], out, first)
 
-    @pl.loop(0, major)
-    def _(d):
-        send(maps_out, maps_pair.at[d], fwd_send.at[d], fwd_recv.at[d], partner).wait_recv()
+    if major > 1:
+        map_copy(via).start()
+    for d in range(1, major):
+        if d != via:
+            cross_copy(d).start()
+            map_copy(d).start()
+    cross_copy(0).start()
+    apply(held, me * group, maps, out, me * group)
+    if major > 1:
+        map_copy(via).wait_recv()
+        cross_copy(via).start()
+        take(via)
+
+    @pl.loop(0, major - 2)
+    def _(i):
+        d = lax.rem(via + i, major - 1) + 1
+        map_copy(d).wait_recv()
+        take(d)
+
+    for d in range(major):
+        cross_copy(d).wait_recv()
 
     for d in range(major):
         pair_copy(d).wait_send()
-        fwd_copy(d).wait_send()
+        cross_copy(d).wait_send()
         if d > 0:
             sum_copy(d).wait_send()
             map_copy(d).wait_send()

time: 27.8 us -> 26.9 us (0.968)
  Pallas kernels: 27.7 us -> 26.7 us
    pallas_call x1, Pallas kernels: 24.7 us -> 23.8 us  [local(): pl.pallas_call(functools.partial(main_kernel, n), out_shape=[jax.ShapeDty...]
where the time goes in v4:
time: 26.9 us; the launch traced here: 26.7 us
  Pallas kernels  26.7 us (99%)
    pallas_call x1, Pallas kernels, local(): pl.pallas_call(functools.partial(main_kernel, n), out_shape=[jax.ShapeDty...  23.8 us
    pallas_call x1, Pallas kernels, local(): pl.pallas_call(functools.partial(finish_kernel, n), out_shape=jax.ShapeDt...  2.93 us

profile of v4, /device:TPU:0, one launch (start us, length us, event | category | flops | bytes accessed | tf_op | source)
XLA Modules:
  0.0 26.7 jit_solution(11088252207131062588)
XLA Ops:
  0.0 23.8 %polar_shapes.1 = (bf16[16,5,256,128]{3,2,1,0:T(8,128)(2,1)S(1)}, bf16[16,5,256,128]{3,2,1,0:T(8,128)(2,1)S(1)}, f32[4,64,128]{2,1,0:T(8,128)S(1)}) custom-call(bf16[16,5,256,128]{3,2,1,0:T(8,128)(2,1)} %spectra.1, f32[1,256]{1,0:T(1,128)} %bitcast.1), custom_call_target="tpu_custom_call" | custom-call | tf_op jit(solution)/shard_map/polar_shapes/pallas_call | solution.py:340
  23.8 2.9 %finish_shapes.1 = bf16[16,5,256,128]{3,2,1,0:T(8,128)(2,1)} custom-call(bf16[16,5,256,128]{3,2,1,0:T(8,128)(2,1)S(1)} %get-tuple-element.8.shapes, bf16[16,5,256,128]{3,2,1,0:T(8,128)(2,1)S(1)} %get-tuple-element.9.held, f32[4,64,128]{2,1,0:T(8,128)S(1)} %get-tuple-element.10.maps_pair), custom_call_target="tpu_custom_call" | custom-call | tf_op jit(solution)/shard_map/finish_shapes/pallas_call | solution.py:377

commit v5 on v4

--- a/solution.py
+++ b/solution.py
@@ -36,16 +36,21 @@
     rolled = pltpu.roll(packed, half, 1)
     top = jnp.where(left, packed, rolled)
     bottom = jnp.where(left, rolled, packed)
-    full = jnp.concatenate([top, bottom, top, bottom], 0)
-    flipped = full.T
+    full = jnp.concatenate([top, bottom], 0)
+    flipped = jnp.concatenate([full, full], 0).T[:half]
     row, lane = places(full.shape)
-    row_left, lane_left = row < half, lane < half
-    i = jnp.where(row_left, row, row - half)
-    j = jnp.where(lane_left, lane, lane - half)
-    real = jnp.where(j >= i, full, flipped)
-    imag = jnp.where(j < i, full, jnp.where(j > i, -flipped, 0.0))
-    imag = jnp.where(row_left, imag, -imag)
-    return jnp.where(jnp.logical_xor(row_left, lane_left), imag, real)
+    left = lane < half
+    j = jnp.where(left, lane, lane - half)
+    real = jnp.where(j >= row, full, flipped)
+    imag = jnp.where(j < row, full, jnp.where(j > row, -flipped, 0.0))
+    return jnp.where(left, real, imag)
+
+
+def complete(top):
+    half = top.shape[0]
+    rolled = pltpu.roll(top, half, 1)
+    lane = places(top.shape)[1]
+    return jnp.concatenate([top, jnp.where(lane < half, -rolled, rolled)], 0)
 
 
 def split(a):
@@ -65,15 +70,16 @@
 
 
 def polar_map(crosses):
-    order = crosses[0].shape[0]
-    row, lane = places((order, order))
+    half = crosses[0].shape[0]
+    row, lane = places(crosses[0].shape)
     eye = row == lane
-    traces = [jnp.sum(jnp.where(eye, c, 0.0), keepdims=True) for c in crosses]
+    traces = [2.0 * jnp.sum(jnp.where(eye, c, 0.0), keepdims=True) for c in crosses]
     grams = [c / t for c, t in zip(crosses, traces)]
     maps = [jnp.where(eye, 1.5 - 0.5 * g, -0.5 * g) for g in grams]
     for step in range(NS_STEPS):
-        lefts = [left_form(g) for g in grams]
-        rights = [jnp.concatenate([g, g], 0) for g in lefts]
+        fulls = [left_form(complete(g)) for g in grams]
+        lefts = [g[:half] for g in fulls]
+        rights = [jnp.concatenate([g, g], 0) for g in fulls]
         if step == 0:
             squares = [product(g, r) for g, r in zip(lefts, rights)]
         elif step < NS_STEPS - 1:
@@ -81,8 +87,8 @@
                 product(jnp.concatenate([g, left_form(q)], 0), r)
                 for g, q, r in zip(lefts, maps, rights)
             ]
-            squares = [x[:order] for x in both]
-            maps = [1.5 * q - 0.5 * x[order:] for q, x in zip(maps, both)]
+            squares = [x[:half] for x in both]
+            maps = [1.5 * q - 0.5 * x[half:] for q, x in zip(maps, both)]
         else:
             maps = [1.5 * q - 0.5 * product(left_form(q), r) for q, r in zip(maps, rights)]
         if step < NS_STEPS - 1:
@@ -96,7 +102,7 @@
 def apply(held, first, maps, out, place):
     group = len(maps)
     _, var_count, points, cols = held.shape
-    maps = [m.astype(jnp.bfloat16) for m in maps]
+    maps = [complete(m).astype(jnp.bfloat16) for m in maps]
     if group == 2:
         zero = jnp.zeros((cols, cols), jnp.bfloat16)
         right = jnp.concatenate(
@@ -262,7 +268,7 @@
 
     maps = polar_map([unpack(o) for o in own])
     for j in range(group):
-        maps_out[part(j)] = pack(maps[j][:half])
+        maps_out[part(j)] = pack(maps[j])
     def take(d):
         first = (behind(d) * 2 + b) * group
         apply(held, first, [unpack(maps_in[d - 1, part(j)]) for j in range(group)], out, first)

time: 26.9 us -> 27.6 us (1.026)
  Pallas kernels: 26.7 us -> 27.5 us
    pallas_call x1, Pallas kernels: 23.8 us -> 24.3 us  [local(): pl.pallas_call(functools.partial(main_kernel, n), out_shape=[jax.ShapeDty...]
where the time goes in v5:
time: 27.6 us; the launch traced here: 27.5 us
  Pallas kernels  27.5 us (100%)
    pallas_call x1, Pallas kernels, local(): pl.pallas_call(functools.partial(main_kernel, n), out_shape=[jax.ShapeDty...  24.3 us
    pallas_call x1, Pallas kernels, local(): pl.pallas_call(functools.partial(finish_kernel, n), out_shape=jax.ShapeDt...  3.14 us

profile of v5, /device:TPU:0, one launch (start us, length us, event | category | flops | bytes accessed | tf_op | source)
XLA Modules:
  0.0 27.5 jit_solution(3748130525313035176)
XLA Ops:
  0.0 24.3 %polar_shapes.1 = (bf16[16,5,256,128]{3,2,1,0:T(8,128)(2,1)S(1)}, bf16[16,5,256,128]{3,2,1,0:T(8,128)(2,1)S(1)}, f32[4,64,128]{2,1,0:T(8,128)S(1)}) custom-call(bf16[16,5,256,128]{3,2,1,0:T(8,128)(2,1)} %spectra.1, f32[1,256]{1,0:T(1,128)} %bitcast.1), custom_call_target="tpu_custom_call" | custom-call | tf_op jit(solution)/shard_map/polar_shapes/pallas_call | solution.py:346
  24.4 3.1 %finish_shapes.1 = bf16[16,5,256,128]{3,2,1,0:T(8,128)(2,1)} custom-call(bf16[16,5,256,128]{3,2,1,0:T(8,128)(2,1)S(1)} %get-tuple-element.8.shapes, bf16[16,5,256,128]{3,2,1,0:T(8,128)(2,1)S(1)} %get-tuple-element.9.held, f32[4,64,128]{2,1,0:T(8,128)S(1)} %get-tuple-element.10.maps_pair), custom_call_target="tpu_custom_call" | custom-call | tf_op jit(solution)/shard_map/finish_shapes/pallas_call | solution.py:383

commit v6 on v4

v6 whole, which is shorter than its diff:
```python
import functools

import jax
import jax.numpy as jnp
from jax import lax
from jax.experimental import pallas as pl
from jax.experimental.pallas import tpu as pltpu
from jax.sharding import PartitionSpec as P

NS_STEPS = 10
MESH = pl.DeviceIdType.MESH


def places(shape):
    return (
        lax.broadcasted_iota(jnp.int32, shape, 0),
        lax.broadcasted_iota(jnp.int32, shape, 1),
    )


def pack(top):
    half, cols = top.shape
    row, lane = places(top.shape)
    left = lane < half
    upper = jnp.where(left, lane, lane - half) >= row
    rolled = pltpu.roll(top, half, 1)
    both = jnp.where(jnp.logical_xor(left, upper), rolled, top)
    quarter = half // 2
    return jnp.where(left[:quarter], both[:quarter], both[quarter:])


def unpack(packed):
    quarter, cols = packed.shape
    half = 2 * quarter
    left = places(packed.shape)[1] < half
    rolled = pltpu.roll(packed, half, 1)
    top = jnp.where(left, packed, rolled)
    bottom = jnp.where(left, rolled, packed)
    full = jnp.concatenate([top, bottom, top, bottom], 0)
    flipped = full.T
    row, lane = places(full.shape)
    row_left, lane_left = row < half, lane < half
    i = jnp.where(row_left, row, row - half)
    j = jnp.where(lane_left, lane, lane - half)
    real = jnp.where(j >= i, full, flipped)
    imag = jnp.where(j < i, full, jnp.where(j > i, -flipped, 0.0))
    imag = jnp.where(row_left, imag, -imag)
    return jnp.where(jnp.logical_xor(row_left, lane_left), imag, real)


def split(a):
    high = a.astype(jnp.bfloat16)
    low = (a - high.astype(jnp.float32)).astype(jnp.bfloat16)
    return high, low


def left_form(a):
    return jnp.concatenate(split(a), 1)


def product(left, right):
    wide = jnp.dot(left, right, preferred_element_type=jnp.float32)
    cols = wide.shape[1] // 2
    return wide[:, :cols] + wide[:, cols:]


def polar_map(crosses):
    order = crosses[0].shape[0]
    row, lane = places((order, order))
    eye = row == lane
    traces = [jnp.sum(jnp.where(eye, c, 0.0), keepdims=True) for c in crosses]
    grams = [c / t for c, t in zip(crosses, traces)]
    maps = [jnp.where(eye, 1.5 - 0.5 * g, -0.5 * g) for g in grams]
    for step in range(NS_STEPS):
        lefts = [left_form(g) for g in grams]
        rights = [jnp.concatenate([g, g], 0) for g in lefts]
        if step == 0:
            squares = [product(g, r) for g, r in zip(lefts, rights)]
        elif step < NS_STEPS - 1:
            both = [
                product(jnp.concatenate([g, left_form(q)], 0), r)
                for g, q, r in zip(lefts, maps, rights)
            ]
            squares = [x[:order] for x in both]
            maps = [1.5 * q - 0.5 * x[order:] for q, x in zip(maps, both)]
        else:
            maps = [1.5 * q - 0.5 * product(left_form(q), r) for q, r in zip(maps, rights)]
        if step < NS_STEPS - 1:
            halves = [1.5 * g - 0.5 * x for g, x in zip(grams, squares)]
            grams = [
                1.5 * t - 0.5 * product(left_form(t), r) for t, r in zip(halves, rights)
            ]
    return [q * lax.rsqrt(t) for q, t in zip(maps, traces)]


def apply(held, first, maps, out, place):
    group = len(maps)
    _, var_count, points, cols = held.shape
    maps = [m.astype(jnp.bfloat16) for m in maps]
    if group == 2:
        zero = jnp.zeros((cols, cols), jnp.bfloat16)
        right = jnp.concatenate(
            [
                jnp.concatenate([maps[0], zero], 1),
                jnp.concatenate([zero, maps[1]], 1),
            ],
            0,
        )
        for v in range(var_count):
            left = jnp.concatenate([held[first, v], held[first + 1, v]], 1)
            wide = jnp.dot(left, right, preferred_element_type=jnp.float32).astype(out.dtype)
            out[place, v] = wide[:, :cols]
            out[place + 1, v] = wide[:, cols:]
    else:
        for j in range(group):
            for v in range(var_count):
                out[place + j, v] = jnp.dot(
                    held[first + j, v], maps[j], preferred_element_type=jnp.float32
                ).astype(out.dtype)


def offset(n, i):
    return lax.rem(n // 2 - 1 + i, n - 1) + 1


def main_kernel(
    n, late, spectra, weights, out, held, maps_in, row_weights, root, sums_out, sums_in, maps_out,
    load_sem, weight_sem, sum_send, sum_recv, map_send, map_recv,
):
    me = lax.axis_index("pts")
    _, var_count, points, cols = held.shape
    group = held.shape[0] // n
    half = cols // 2
    quarter = half // 2

    def peer(i):
        return lax.rem(me + offset(n, i), n)

    def load(i):
        owner = me if isinstance(i, int) and i == n - 1 else peer(i)
        rows = pl.ds(owner * group, group)
        return pltpu.make_async_copy(spectra.at[rows], held.at[rows], load_sem.at[i])

    def sum_copy(i):
        return pltpu.make_async_remote_copy(
            src_ref=sums_out.at[i], dst_ref=sums_in.at[i], send_sem=sum_send.at[i],
            recv_sem=sum_recv.at[i], device_id={"pts": peer(i)}, device_id_type=MESH,
        )

    def map_copy(i):
        return pltpu.make_async_remote_copy(
            src_ref=maps_out, dst_ref=maps_in.at[i], send_sem=map_send.at[i],
            recv_sem=map_recv.at[i], device_id={"pts": peer(i)}, device_id_type=MESH,
        )

    barrier = pltpu.get_barrier_semaphore()
    for i in range(n - 1):
        pl.semaphore_signal(barrier, inc=1, device_id={"pts": peer(i)}, device_id_type=MESH)
    weight_copy = pltpu.make_async_copy(weights, row_weights, weight_sem)
    weight_copy.start()
    for i in range(n):
        load(i).start()
    weight_copy.wait()
    root[...] = jnp.broadcast_to(jnp.sqrt(row_weights[...]), (cols, points)).T

    def fold(total):
        top, bottom = total[:half], pltpu.roll(total[half:], half, 1)
        lane = places(top.shape)[1]
        return pack(top + jnp.where(lane < half, bottom, -bottom))

    def packed_sums(first):
        sums = []
        for start in range(0, group, 2):
            count = min(2, group - start)
            rows = jnp.concatenate(
                [
                    (held[first + start + j].astype(jnp.float32) * root[...])
                    .astype(jnp.bfloat16)
                    .reshape(var_count * points, cols)
                    for j in range(count)
                ],
                1,
            )
            total = lax.dot_general(
                rows, rows, (((0,), (0,)), ((), ())), preferred_element_type=jnp.float32
            )
            for j in range(count):
                own_cols = slice(j * cols, (j + 1) * cols)
                sums.append(fold(total[own_cols, own_cols]))
        return sums

    def part(j):
        return pl.ds(j * quarter, quarter)

    def peer_sums(i):
        load(i).wait()
        for j, packed in enumerate(packed_sums(peer(i) * group)):
            sums_out[i, part(j)] = packed

    early = min(2, n - 1)

    @pl.loop(0, early)
    def _(i):
        peer_sums(i)

    pl.semaphore_wait(barrier, n - 1)
    for i in range(early):
        sum_copy(i).start()

    @pl.loop(early, n - 1)
    def _(i):
        peer_sums(i)
        sum_copy(i).start()

    load(n - 1).wait()
    own = packed_sums(me * group)
    for i in range(n - 1):
        sum_copy(i).wait_recv()
        for j in range(group):
            own[j] = own[j] + sums_in[i, part(j)]

    maps = polar_map([unpack(o) for o in own])
    for j in range(group):
        maps_out[part(j)] = pack(maps[j][:half])
    for i in range(n - 1):
        map_copy(i).start()
    apply(held, me * group, maps, out, me * group)

    @pl.loop(0, n - 1 - late)
    def _(i):
        map_copy(i).wait_recv()
        first = lax.rem(me + n - offset(n, i), n) * group
        apply(held, first, [unpack(maps_in[i, part(j)]) for j in range(group)], out, first)

    for i in range(n - 1 - late, n - 1):
        map_copy(i).wait_recv()
    for i in range(n - 1):
        sum_copy(i).wait_send()
        map_copy(i).wait_send()


def finish_kernel(n, late, shapes, held, maps_in, out, late_shapes, early_sem, late_sem):
    me = lax.axis_index("pts")
    group = held.shape[0] // n
    quarter = maps_in.shape[1] // group
    early = n - 1 - late

    def first(i):
        return lax.rem(me + n - offset(n, i), n) * group

    def early_copy(i):
        rows = pl.ds(me * group if i == early else first(i), group)
        return pltpu.make_async_copy(shapes.at[rows], out.at[rows], early_sem.at[i])

    def late_copy(i):
        return pltpu.make_async_copy(
            late_shapes.at[pl.ds(i * group, group)],
            out.at[pl.ds(first(early + i), group)],
            late_sem.at[i],
        )

    for i in range(early + 1):
        early_copy(i).start()

    @pl.loop(0, late)
    def _(i):
        slot = early + i
        maps = [unpack(maps_in[slot, pl.ds(j * quarter, quarter)]) for j in range(group)]
        apply(held, first(slot), maps, late_shapes, i * group)
        late_copy(i).start()

    for i in range(early + 1):
        early_copy(i).wait()
    for i in range(late):
        late_copy(i).wait()


def local(n, spectra, weights):
    freq_count, var_count, points, cols = spectra.shape
    group = freq_count // n
    slots = (n - 1, group * (cols // 4), cols)
    late = max(1, n // 2 - 1)
    dma = pltpu.SemaphoreType.DMA
    params = dict(vmem_limit_bytes=32 * 1024 * 1024)
    shapes, held, maps_in = pl.pallas_call(
        functools.partial(main_kernel, n, late),
        out_shape=[
            jax.ShapeDtypeStruct(spectra.shape, jnp.bfloat16),
            jax.ShapeDtypeStruct(spectra.shape, jnp.bfloat16),
            jax.ShapeDtypeStruct(slots, jnp.float32),
        ],
        in_specs=[pl.BlockSpec(memory_space=pltpu.HBM)] * 2,
        out_specs=[pl.BlockSpec(memory_space=pltpu.VMEM)] * 3,
        scratch_shapes=[
            pltpu.VMEM((1, points), jnp.float32),
            pltpu.VMEM((points, cols), jnp.float32),
            pltpu.VMEM(slots, jnp.float32),
            pltpu.VMEM(slots, jnp.float32),
            pltpu.VMEM(slots[1:], jnp.float32),
            dma((n,)),
            dma,
            dma((n - 1,)),
            dma((n - 1,)),
            dma((n - 1,)),
            dma((n - 1,)),
        ],
        compiler_params=pltpu.CompilerParams(collective_id=0, has_side_effects=True, **params),
        name="polar_shapes",
    )(
        pltpu.with_memory_space_constraint(spectra, pltpu.HBM),
        pltpu.with_memory_space_constraint(weights.reshape(1, points), pltpu.HBM),
    )
    return pl.pallas_call(
        functools.partial(finish_kernel, n, late),
        out_shape=jax.ShapeDtypeStruct(spectra.shape, jnp.bfloat16),
        in_specs=[pl.BlockSpec(memory_space=pltpu.VMEM)] * 3,
        out_specs=pl.BlockSpec(memory_space=pltpu.HBM),
        scratch_shapes=[
            pltpu.VMEM((late * group, *spectra.shape[1:]), jnp.bfloat16),
            dma((n - late,)),
            dma((late,)),
        ],
        compiler_params=pltpu.CompilerParams(**params),
        name="finish_shapes",
    )(shapes, held, maps_in)


def solution(mesh):
    in_specs = (P("freq", None, "pts", None), P("pts"))
    out_specs = P("freq", None, "pts", None)
    return jax.shard_map(
        functools.partial(local, mesh.shape["pts"]),
        mesh=mesh, in_specs=in_specs, out_specs=out_specs, check_vma=False,
    )
```

time: 26.9 us -> 27.1 us (level)
  Pallas kernels: 26.7 us -> 27 us
where the time goes in v6:
time: 27.1 us; the launch traced here: 27 us
  Pallas kernels  27 us (100%)
    pallas_call x1, Pallas kernels, local(): pl.pallas_call(functools.partial(main_kernel, n, late), out_shape=[jax.Sh...  24.6 us
    pallas_call x1, Pallas kernels, local(): pl.pallas_call(functools.partial(finish_kernel, n, late), out_shape=jax.S...  2.43 us

profile of v6, /device:TPU:0, one launch (start us, length us, event | category | flops | bytes accessed | tf_op | source)
XLA Modules:
  0.0 27.0 jit_solution(7319483841601028820)
XLA Ops:
  0.0 24.6 %polar_shapes.1 = (bf16[16,5,256,128]{3,2,1,0:T(8,128)(2,1)S(1)}, bf16[16,5,256,128]{3,2,1,0:T(8,128)(2,1)S(1)}, f32[7,64,128]{2,1,0:T(8,128)S(1)}) custom-call(bf16[16,5,256,128]{3,2,1,0:T(8,128)(2,1)} %spectra.1, f32[1,256]{1,0:T(1,128)} %bitcast.1), custom_call_target="tpu_custom_call" | custom-call | tf_op jit(solution)/shard_map/polar_shapes/pallas_call | solution.py:285
  24.6 2.4 %finish_shapes.1 = bf16[16,5,256,128]{3,2,1,0:T(8,128)(2,1)} custom-call(bf16[16,5,256,128]{3,2,1,0:T(8,128)(2,1)S(1)} %get-tuple-element.8.shapes, bf16[16,5,256,128]{3,2,1,0:T(8,128)(2,1)S(1)} %get-tuple-element.9.held, f32[7,64,128]{2,1,0:T(8,128)S(1)} %get-tuple-element.10.maps_in), custom_call_target="tpu_custom_call" | custom-call | tf_op jit(solution)/shard_map/finish_shapes/pallas_call | solution.py:313

commit v7 on v4

--- a/solution.py
+++ b/solution.py
@@ -122,7 +122,7 @@
 def main_kernel(
     n, spectra, weights, out, held, maps_pair, row_weights, root, pair_out, pair_in, sums_out,
     sums_in, maps_out, maps_in, load_sem, weight_sem, pair_send, pair_recv, sum_send, sum_recv,
-    map_send, map_recv, fwd_send, fwd_recv,
+    map_send, map_recv, cross_send, cross_recv,
 ):
     major = n // 2
     me = lax.axis_index("pts")
@@ -165,12 +165,9 @@
             maps_out, maps_in.at[d - 1], map_send.at[d - 1], map_recv.at[d - 1], ahead(d) * 2 + b
         )
 
-    via = major // 2
-
     def cross_copy(d):
-        src = maps_in.at[d - 1] if d == via and d > 0 else maps_out
-        target = partner if d == via else ahead(d) * 2 + other
-        return send(src, maps_pair.at[d], fwd_send.at[d], fwd_recv.at[d], target)
+        src = maps_in.at[d - 1] if d > 0 else maps_out
+        return send(src, maps_pair.at[d], cross_send.at[d], cross_recv.at[d], partner)
 
     barrier = pltpu.get_barrier_semaphore()
     pl.semaphore_signal(barrier, inc=1, device_id={"pts": partner}, device_id_type=MESH)
@@ -178,11 +175,6 @@
         pl.semaphore_signal(
             barrier, inc=1, device_id={"pts": ahead(d) * 2 + b}, device_id_type=MESH
         )
-    for d in range(1, major):
-        if d != via:
-            pl.semaphore_signal(
-                barrier, inc=1, device_id={"pts": ahead(d) * 2 + other}, device_id_type=MESH
-            )
     weight_copy = pltpu.make_async_copy(weights, row_weights, weight_sem)
     weight_copy.start()
     for side in (1, 0):
@@ -231,7 +223,7 @@
     def _(i):
         pair_sums(lax.rem(i + 1, major))
 
-    pl.semaphore_wait(barrier, major + max(major - 2, 0))
+    pl.semaphore_wait(barrier, major)
     for i in range(early):
         pair_copy((i + 1) % major).start()
 
@@ -263,30 +255,24 @@
     maps = polar_map([unpack(o) for o in own])
     for j in range(group):
         maps_out[part(j)] = pack(maps[j][:half])
-    def take(d):
+    order = sorted(range(1, major), key=lambda d: abs(d - major // 2))
+    for d in order:
+        map_copy(d).start()
+    cross_copy(0).start()
+    apply(held, me * group, maps, out, me * group)
+    for d in order:
+        map_copy(d).wait_recv()
+        cross_copy(d).start()
+
+    @pl.loop(1, major)
+    def _(d):
         first = (behind(d) * 2 + b) * group
         apply(held, first, [unpack(maps_in[d - 1, part(j)]) for j in range(group)], out, first)
 
-    if major > 1:
-        map_copy(via).start()
-    for d in range(1, major):
-        if d != via:
-            cross_copy(d).start()
-            map_copy(d).start()
-    cross_copy(0).start()
-    apply(held, me * group, maps, out, me * group)
-    if major > 1:
-        map_copy(via).wait_recv()
-        cross_copy(via).start()
-        take(via)
-
-    @pl.loop(0, major - 2)
-    def _(i):
-        d = lax.rem(via + i, major - 1) + 1
-        map_copy(d).wait_recv()
-        take(d)
-
-    for d in range(major):
+    cross_copy(0).wait_recv()
+    first = partner * group
+    apply(held, first, [unpack(maps_pair[0, part(j)]) for j in range(group)], out, first)
+    for d in order:
         cross_copy(d).wait_recv()
 
     for d in range(major):
@@ -313,22 +299,27 @@
 
     def late_copy(d):
         return pltpu.make_async_copy(
-            late.at[pl.ds(d * group, group)],
+            late.at[pl.ds((d - 1) * group, group)],
             out.at[pl.ds(late_first(d), group)],
             late_sem.at[d],
         )
 
+    pair_rows = pl.ds(late_first(0), group)
+    pair_copy = pltpu.make_async_copy(shapes.at[pair_rows], out.at[pair_rows], late_sem.at[0])
     for d in range(major):
         early_copy(d).start()
-
-    @pl.loop(0, major)
+    pair_copy.start()
+
+    @pl.loop(1, major)
     def _(d):
         maps = [unpack(maps_pair[d, pl.ds(j * quarter, quarter)]) for j in range(group)]
-        apply(held, late_first(d), maps, late, d * group)
+        apply(held, late_first(d), maps, late, (d - 1) * group)
         late_copy(d).start()
 
     for d in range(major):
         early_copy(d).wait()
+    pair_copy.wait()
+    for d in range(1, major):
         late_copy(d).wait()
 
 
@@ -380,7 +371,7 @@
         in_specs=[pl.BlockSpec(memory_space=pltpu.VMEM)] * 3,
         out_specs=pl.BlockSpec(memory_space=pltpu.HBM),
         scratch_shapes=[
-            pltpu.VMEM((freq_count // 2, *spectra.shape[1:]), jnp.bfloat16),
+            pltpu.VMEM((max(1, freq_count // 2 - freq_count // n), *spectra.shape[1:]), jnp.bfloat16),
             dma((major,)),
             dma((major,)),
         ],

time: 26.9 us -> 27.5 us (1.022)
  Pallas kernels: 26.7 us -> 27.4 us
    pallas_call x1, Pallas kernels: 23.8 us -> 24.9 us  [local(): pl.pallas_call(functools.partial(main_kernel, n), out_shape=[jax.ShapeDty...]
    pallas_call x1, Pallas kernels: 2.93 us -> 2.44 us  [local(): pl.pallas_call(functools.partial(finish_kernel, n), out_shape=jax.ShapeDt...]
where the time goes in v7:
time: 27.5 us; the launch traced here: 27.4 us
  Pallas kernels  27.4 us (100%)
    pallas_call x1, Pallas kernels, local(): pl.pallas_call(functools.partial(main_kernel, n), out_shape=[jax.ShapeDty...  24.9 us
    pallas_call x1, Pallas kernels, local(): pl.pallas_call(functools.partial(finish_kernel, n), out_shape=jax.ShapeDt...  2.44 us

profile of v7, /device:TPU:0, one launch (start us, length us, event | category | flops | bytes accessed | tf_op | source)
XLA Modules:
  0.0 27.4 jit_solution(13503482822672577321)
XLA Ops:
  0.0 24.9 %polar_shapes.1 = (bf16[16,5,256,128]{3,2,1,0:T(8,128)(2,1)S(1)}, bf16[16,5,256,128]{3,2,1,0:T(8,128)(2,1)S(1)}, f32[4,64,128]{2,1,0:T(8,128)S(1)}) custom-call(bf16[16,5,256,128]{3,2,1,0:T(8,128)(2,1)} %spectra.1, f32[1,256]{1,0:T(1,128)} %bitcast.1), custom_call_target="tpu_custom_call" | custom-call | tf_op jit(solution)/shard_map/polar_shapes/pallas_call | solution.py:331
  24.9 2.4 %finish_shapes.1 = bf16[16,5,256,128]{3,2,1,0:T(8,128)(2,1)} custom-call(bf16[16,5,256,128]{3,2,1,0:T(8,128)(2,1)S(1)} %get-tuple-element.8.shapes, bf16[16,5,256,128]{3,2,1,0:T(8,128)(2,1)S(1)} %get-tuple-element.9.held, f32[4,64,128]{2,1,0:T(8,128)S(1)} %get-tuple-element.10.maps_pair), custom_call_target="tpu_custom_call" | custom-call | tf_op jit(solution)/shard_map/finish_shapes/pallas_call | solution.py:368

commit v8 on v4

--- a/solution.py
+++ b/solution.py
@@ -122,7 +122,7 @@
 def main_kernel(
     n, spectra, weights, out, held, maps_pair, row_weights, root, pair_out, pair_in, sums_out,
     sums_in, maps_out, maps_in, load_sem, weight_sem, pair_send, pair_recv, sum_send, sum_recv,
-    map_send, map_recv, fwd_send, fwd_recv,
+    map_send, map_recv, cross_send, cross_recv,
 ):
     major = n // 2
     me = lax.axis_index("pts")
@@ -170,7 +170,7 @@
     def cross_copy(d):
         src = maps_in.at[d - 1] if d == via and d > 0 else maps_out
         target = partner if d == via else ahead(d) * 2 + other
-        return send(src, maps_pair.at[d], fwd_send.at[d], fwd_recv.at[d], target)
+        return send(src, maps_pair.at[d], cross_send.at[d], cross_recv.at[d], target)
 
     barrier = pltpu.get_barrier_semaphore()
     pl.semaphore_signal(barrier, inc=1, device_id={"pts": partner}, device_id_type=MESH)
@@ -286,7 +286,10 @@
         map_copy(d).wait_recv()
         take(d)
 
-    for d in range(major):
+    cross_copy(0).wait_recv()
+    first = partner * group
+    apply(held, first, [unpack(maps_pair[0, part(j)]) for j in range(group)], out, first)
+    for d in range(1, major):
         cross_copy(d).wait_recv()
 
     for d in range(major):
@@ -313,22 +316,27 @@
 
     def late_copy(d):
         return pltpu.make_async_copy(
-            late.at[pl.ds(d * group, group)],
+            late.at[pl.ds((d - 1) * group, group)],
             out.at[pl.ds(late_first(d), group)],
             late_sem.at[d],
         )
 
+    pair_rows = pl.ds(late_first(0), group)
+    pair_copy = pltpu.make_async_copy(shapes.at[pair_rows], out.at[pair_rows], late_sem.at[0])
     for d in range(major):
         early_copy(d).start()
-
-    @pl.loop(0, major)
+    pair_copy.start()
+
+    @pl.loop(1, major)
     def _(d):
         maps = [unpack(maps_pair[d, pl.ds(j * quarter, quarter)]) for j in range(group)]
-        apply(held, late_first(d), maps, late, d * group)
+        apply(held, late_first(d), maps, late, (d - 1) * group)
         late_copy(d).start()
 
     for d in range(major):
         early_copy(d).wait()
+    pair_copy.wait()
+    for d in range(1, major):
         late_copy(d).wait()
 
 
@@ -380,7 +388,7 @@
         in_specs=[pl.BlockSpec(memory_space=pltpu.VMEM)] * 3,
         out_specs=pl.BlockSpec(memory_space=pltpu.HBM),
         scratch_shapes=[
-            pltpu.VMEM((freq_count // 2, *spectra.shape[1:]), jnp.bfloat16),
+            pltpu.VMEM((max(1, freq_count // 2 - freq_count // n), *spectra.shape[1:]), jnp.bfloat16),
             dma((major,)),
             dma((major,)),
         ],

time: 26.9 us -> 26.8 us (level)
    pallas_call x1, Pallas kernels: 2.93 us -> 2.44 us  [local(): pl.pallas_call(functools.partial(finish_kernel, n), out_shape=jax.ShapeDt...]
    pallas_call x1, Pallas kernels: 23.8 us -> 24.2 us  [local(): pl.pallas_call(functools.partial(main_kernel, n), out_shape=[jax.ShapeDty...]
where the time goes in v8:
time: 26.8 us; the launch traced here: 26.7 us
  Pallas kernels  26.7 us (100%)
    pallas_call x1, Pallas kernels, local(): pl.pallas_call(functools.partial(main_kernel, n), out_shape=[jax.ShapeDty...  24.2 us
    pallas_call x1, Pallas kernels, local(): pl.pallas_call(functools.partial(finish_kernel, n), out_shape=jax.ShapeDt...  2.44 us

profile of v8, /device:TPU:0, one launch (start us, length us, event | category | flops | bytes accessed | tf_op | source)
XLA Modules:
  0.0 26.7 jit_solution(10951949525797874343)
XLA Ops:
  0.0 24.2 %polar_shapes.1 = (bf16[16,5,256,128]{3,2,1,0:T(8,128)(2,1)S(1)}, bf16[16,5,256,128]{3,2,1,0:T(8,128)(2,1)S(1)}, f32[4,64,128]{2,1,0:T(8,128)S(1)}) custom-call(bf16[16,5,256,128]{3,2,1,0:T(8,128)(2,1)} %spectra.1, f32[1,256]{1,0:T(1,128)} %bitcast.1), custom_call_target="tpu_custom_call" | custom-call | tf_op jit(solution)/shard_map/polar_shapes/pallas_call | solution.py:348
  24.2 2.4 %finish_shapes.1 = bf16[16,5,256,128]{3,2,1,0:T(8,128)(2,1)} custom-call(bf16[16,5,256,128]{3,2,1,0:T(8,128)(2,1)S(1)} %get-tuple-element.8.shapes, bf16[16,5,256,128]{3,2,1,0:T(8,128)(2,1)S(1)} %get-tuple-element.9.held, f32[4,64,128]{2,1,0:T(8,128)S(1)} %get-tuple-element.10.maps_pair), custom_call_target="tpu_custom_call" | custom-call | tf_op jit(solution)/shard_map/finish_shapes/pallas_call | solution.py:385

commit v9 on v8

--- a/solution.py
+++ b/solution.py
@@ -185,11 +185,13 @@
             )
     weight_copy = pltpu.make_async_copy(weights, row_weights, weight_sem)
     weight_copy.start()
-    for side in (1, 0):
-        for d in range(1, major + 1):
-            load(d % major, side).start()
+    loads = [load(d % major, side) for side in (1, 0) for d in range(1, major + 1)]
+    for copy in loads[:2]:
+        copy.start()
     weight_copy.wait()
     root[...] = jnp.broadcast_to(jnp.sqrt(row_weights[...]), (cols, points)).T
+    for copy in loads[2:]:
+        copy.start()
 
     def fold(total):
         top, bottom = total[:half], pltpu.roll(total[half:], half, 1)

time: 26.8 us -> 25.7 us (0.959)
  Pallas kernels: 26.7 us -> 25.6 us
    pallas_call x1, Pallas kernels: 24.2 us -> 23.1 us  [local(): pl.pallas_call(functools.partial(main_kernel, n), out_shape=[jax.ShapeDty...]
where the time goes in v9:
time: 25.7 us; the launch traced here: 25.6 us
  Pallas kernels  25.6 us (100%)
    pallas_call x1, Pallas kernels, local(): pl.pallas_call(functools.partial(main_kernel, n), out_shape=[jax.ShapeDty...  23.1 us
    pallas_call x1, Pallas kernels, local(): pl.pallas_call(functools.partial(finish_kernel, n), out_shape=jax.ShapeDt...  2.44 us

profile of v9, /device:TPU:0, one launch (start us, length us, event | category | flops | bytes accessed | tf_op | source)
XLA Modules:
  0.0 25.6 jit_solution(13663219024129958311)
XLA Ops:
  0.0 23.1 %polar_shapes.1 = (bf16[16,5,256,128]{3,2,1,0:T(8,128)(2,1)S(1)}, bf16[16,5,256,128]{3,2,1,0:T(8,128)(2,1)S(1)}, f32[4,64,128]{2,1,0:T(8,128)S(1)}) custom-call(bf16[16,5,256,128]{3,2,1,0:T(8,128)(2,1)} %spectra.1, f32[1,256]{1,0:T(1,128)} %bitcast.1), custom_call_target="tpu_custom_call" | custom-call | tf_op jit(solution)/shard_map/polar_shapes/pallas_call | solution.py:350
  23.1 2.4 %finish_shapes.1 = bf16[16,5,256,128]{3,2,1,0:T(8,128)(2,1)} custom-call(bf16[16,5,256,128]{3,2,1,0:T(8,128)(2,1)S(1)} %get-tuple-element.8.shapes, bf16[16,5,256,128]{3,2,1,0:T(8,128)(2,1)S(1)} %get-tuple-element.9.held, f32[4,64,128]{2,1,0:T(8,128)S(1)} %get-tuple-element.10.maps_pair), custom_call_target="tpu_custom_call" | custom-call | tf_op jit(solution)/shard_map/finish_shapes/pallas_call | solution.py:387
